TPU v7x, 32 devices: a whole 2x2x4 slice. The times are simulated.
32 devices in a mesh: rep: 2 (over x), gx: 8 (over z, y), gy: 2 (over core).
Axes of the slice: x: 2, y: 2, z: 4, core: 2. Of those that a mesh axis runs over, the one named last changes fastest.
Arguments:
- gate_pre: bfloat16 [2048, 26624], P('rep', ('gx', 'gy')), parts along dimension 0, may hold values from -6 to 6
- up_pre: bfloat16 [2048, 26624], P('rep', ('gx', 'gy')), parts along dimension 0, may hold values from -6 to 6
- down_weight: bfloat16 [26624, 8192], P('gx', 'gy'), may hold values from -0.0546875 to 0.0546875
Outputs:
- layer_out: bfloat16 [2048, 8192], P('rep', ('gy', 'gx')), parts along dimension 0
There are 2 independent parts, one for each index of `rep`. A program takes and returns all parts, laid end to end along the dimension named above; an argument that names none is the same for every part. Nothing has to cross between parts.
All inputs are finite; a program needn't handle non-finite values.
Results may differ from a plain program's by a relative error of at most 0.0049.
Values may be sent and summed in bfloat16 or wider, within the bound.
A program may use at most 128 MiB of HBM per device.

v0:
```python
import jax
import jax.numpy as jnp
from jax import lax
from jax.sharding import PartitionSpec as P


def activate(gate_vals, up_vals):
    return (jax.nn.silu(gate_vals.astype(jnp.float32)) * up_vals.astype(jnp.float32)).astype(
        jnp.bfloat16
    )


def shards(gate_pre, up_pre, down_weight):
    hidden = lax.all_gather(activate(gate_pre, up_pre), "gy", axis=1, tiled=True)
    partial_out = jnp.dot(hidden, down_weight, preferred_element_type=jnp.float32)
    return lax.psum_scatter(partial_out, "gx", scatter_dimension=1, tiled=True).astype(jnp.bfloat16)


def solution(mesh):
    placed = (P("rep", ("gx", "gy")), P("rep", ("gx", "gy")), P("gx", "gy"))
    return jax.shard_map(
        shards, mesh=mesh, in_specs=placed, out_specs=P("rep", ("gy", "gx")), check_vma=False
    )
```

profile of v0, /device:TPU:16, one launch (start us, length us, event | category | flops | bytes accessed | tf_op | source)
XLA Modules:
  0.0 358.3 jit_solution(2289572289691898804)
XLA Ops:
  6.5 0.0 all-gather.2.cloned.1.call-start
  6.5 5.2 %fusion.4 = bf16[1024,1664]{1,0:T(8,128)(2,1)} fusion(bf16[1024,1664]{1,0:T(8,128)(2,1)} %param.4, bf16[1024,1664]{1,0:T(8,128)(2,1)} %param.3), kind=kLoop, calls=%fused_computation.6 | loop fusion | flops 13631488 | bytes 10223616 | tf_op jit(solution)/shard_map/convert_element_type | solution.py:8
  11.8 0.0 all-gather.2.cloned.1.call-update
  11.8 0.0 reduce-scatter.2.cloned.1.call-start
  11.8 18.9 %all-gather.2.cloned.1.call-done = bf16[1024,3328]{1,0:T(8,128)(2,1)} async-done(((bf16[1024,1664]{1,0:T(8,128)(2,1)}), bf16[1024,3328]{1,0:T(8,128)(2,1)}) %all-gather.2.cloned.1.call-update) | async-done | bytes 6815760 | tf_op jit(solution)/shard_map/all_gather | solution.py:14
  30.8 35.6 %fusion.5 = f32[1024,4096]{1,0:T(8,128)} fusion(bf16[1024,3328]{1,0:T(8,128)(2,1)} %all-gather.2.cloned.1.call-done, bf16[3328,4096]{1,0:T(8,128)(2,1)} %param.5), kind=kOutput, calls=%fused_computation.7 | convolution fusion | flops 27917287424 | bytes 50855936 | tf_op jit(solution)/shard_map/dot_general | solution.py:15
  66.3 0.0 reduce-scatter.2.cloned.1.call-update
  66.4 282.4 %reduce-scatter.2.cloned.1.call-done = f32[1024,512]{1,0:T(8,128)} async-done(((f32[1024,4096]{1,0:T(8,128)}), f32[1024,512]{1,0:T(8,128)}) %reduce-scatter.2.cloned.1.call-update) | async-done | bytes 2097168 | tf_op jit(solution)/shard_map/reduce_scatter | solution.py:16
  348.8 2.7 convert_element_type.15
Async XLA Ops:
  6.5 24.2 %all-gather.2.cloned.1.call-start = ((), (), s32[]{:S(2)}) async-start(), calls=%async_computation.1 | async-start | bytes 10223616 | tf_op jit(solution)/shard_map/all_gather | solution.py:14
  11.8 337.0 %reduce-scatter.2.cloned.1.call-start = ((), (), s32[]{:S(2)}) async-start(), calls=%async_computation.2 | async-start | bytes 18874368 | tf_op jit(solution)/shard_map/reduce_scatter | solution.py:16
Sparse Core Ops, SparseCore 0:
  11.9 18.8 all-gather.1
  66.5 282.2 reduce-scatter.1
where the time goes:
time: 361 us; the launch traced here: 358 us
  waiting for transfers between devices  301 us (83%)
  matrix products  35.6 us (10%)
  between operations  13.4 us (4%)
  other arithmetic  7.92 us (2%)
    reduce_scatter x1, waiting for transfers between devices, shards(): lax.psum_scatter(partial_out, 'gx', scatter_dimension=1, tiled=True)  282 us
    dot_general x1, matrix products, shards(): jnp.dot(hidden, down_weight, preferred_element_type=jnp.float32)  35.6 us
    all_gather x1, waiting for transfers between devices, shards(): lax.all_gather(activate(gate_pre, up_pre), 'gy', axis=1, tiled=True)  18.9 us
  transfers between devices with their start and end apart: 2, of which 2 were waited for; matrix products, arithmetic and copies ran while one was open for 0% of the time, Pallas kernels for 0%

commit v1 on v0

v1 whole, which is shorter than its diff:
```python
import functools

import jax
import jax.numpy as jnp
from jax import lax
from jax.experimental import pallas as pl
from jax.experimental.pallas import tpu as pltpu
from jax.sharding import PartitionSpec as P

MESH = pl.DeviceIdType.MESH
WSLOTS = 3
F32 = jnp.float32
BF16 = jnp.bfloat16


def activate(gate_vals, up_vals):
    return (jax.nn.silu(gate_vals.astype(F32)) * up_vals.astype(F32)).astype(BF16)


def plain_shards(gate_pre, up_pre, down_weight):
    hidden = lax.all_gather(activate(gate_pre, up_pre), "gy", axis=1, tiled=True)
    partial_out = jnp.dot(hidden, down_weight, preferred_element_type=F32)
    return lax.psum_scatter(partial_out, "gx", scatter_dimension=1, tiled=True).astype(BF16)


def kernel(
    gate_ref, up_ref, w_ref, out_ref,
    gbuf, ubuf, hid, wbuf, part, ybuf, zlo, zup,
    gsem, usem, wsem, h_send, h_recv,
    y_send, y_recv, up_send, dn_send, zlo_recv, zup_recv,
):
    rows, half = gate_ref.shape
    cols = out_ref.shape[1]
    step = rows // 4
    ch = rows // 8
    core = lax.axis_index("gy")
    g = lax.axis_index("gx")
    z = g // 2
    y = g % 2
    low = z < 2
    end = jnp.logical_or(z == 0, z == 3)
    mid = jnp.logical_not(end)
    ypeer = z * 2 + (1 - y)
    upward = jnp.where(low, g + 2, g - 2)
    downward = jnp.where(low, g - 2, g + 2)

    def owner(i):
        k = jnp.where(end, (3, 2, 1, 0)[i // 2], (3, 0, 2, 1)[i // 2])
        zz = jnp.where(low, k, 3 - k)
        return zz * 2 + (1 - y if i % 2 == 0 else y)

    def load_in(r):
        at = pl.ds(r * step, step)
        return (
            pltpu.make_async_copy(gate_ref.at[at], gbuf.at[at], gsem.at[r]),
            pltpu.make_async_copy(up_ref.at[at], ubuf.at[at], usem.at[r]),
        )

    def load_w(i):
        s = i % WSLOTS
        c = pl.ds(pl.multiple_of(owner(i) * cols, cols), cols)
        mine = pl.ds(pl.multiple_of(core * half, half), half)
        other = pl.ds(pl.multiple_of((1 - core) * half, half), half)
        return (
            pltpu.make_async_copy(w_ref.at[mine, c], wbuf.at[s, pl.ds(0, half)], wsem.at[s, 0]),
            pltpu.make_async_copy(w_ref.at[other, c], wbuf.at[s, pl.ds(half, half)], wsem.at[s, 1]),
        )

    def start(copies):
        for copy in copies:
            copy.start()

    def wait(copies):
        for copy in copies:
            copy.wait()

    def exchange(r):
        at = pl.ds(r * step, step)
        return pltpu.make_async_remote_copy(
            src_ref=hid.at[at, pl.ds(0, half)], dst_ref=hid.at[at, pl.ds(half, half)],
            send_sem=h_send.at[r], recv_sem=h_recv.at[r],
            device_id={"gy": 1 - core}, device_id_type=MESH,
        )

    def chunk(i, n):
        return part.at[i, pl.ds(pl.multiple_of(n * ch, ch), ch)]

    def to_y(i, n, s):
        return pltpu.make_async_remote_copy(
            src_ref=chunk(i, n), dst_ref=ybuf.at[s], send_sem=y_send.at[s], recv_sem=y_recv.at[s],
            device_id={"gx": ypeer}, device_id_type=MESH,
        )

    def end_up(i, n, s):
        return pltpu.make_async_remote_copy(
            src_ref=chunk(i, n), dst_ref=zlo.at[s], send_sem=up_send.at[s], recv_sem=zlo_recv.at[s],
            device_id={"gx": upward}, device_id_type=MESH,
        )

    def mid_up(i, n, s):
        return pltpu.make_async_remote_copy(
            src_ref=chunk(i, n), dst_ref=zup.at[s], send_sem=up_send.at[s], recv_sem=zup_recv.at[s],
            device_id={"gx": upward}, device_id_type=MESH,
        )

    def mid_down(i, n, s):
        return pltpu.make_async_remote_copy(
            src_ref=chunk(i, n), dst_ref=zup.at[s], send_sem=dn_send.at[s], recv_sem=zup_recv.at[s],
            device_id={"gx": downward}, device_id_type=MESH,
        )

    def act(r):
        wait(load_in(r))

        @pl.loop(0, step // 16)
        def _(t):
            at = pl.ds(pl.multiple_of(r * step + t * 16, 16), 16)
            v = gbuf[at, :].astype(F32)
            h = (0.5 * v) * (jnp.tanh(0.5 * v) + 1.0)
            hid[at, pl.ds(0, half)] = (h * ubuf[at, :].astype(F32)).astype(BF16)

    def mm(i, r):
        at = pl.ds(r * step, step) if isinstance(r, int) else pl.ds(pl.multiple_of(r * step, step), step)
        part[i, at, :] = jnp.dot(
            hid[at, :], wbuf[i % WSLOTS], preferred_element_type=F32
        ).astype(BF16)

    def got_y(s):
        to_y(0, 0, s).wait_recv()
        return ybuf[s].astype(F32)

    def got_lo(s):
        end_up(0, 0, s).wait_recv()
        return zlo[s].astype(F32)

    def got_up(s):
        mid_up(0, 0, s).wait_recv()
        return zup[s].astype(F32)

    def total(i, n, *terms):
        at = pl.ds(pl.multiple_of(n * ch, ch), ch)
        value = part[i, at, :].astype(F32)
        for term in terms:
            value = value + term
        return value.astype(BF16)

    def add(i, n, *terms):
        at = pl.ds(pl.multiple_of(n * ch, ch), ch)
        part[i, at, :] = total(i, n, *terms)

    def final(i, n, *terms):
        at = pl.ds(pl.multiple_of(n * ch, ch), ch)
        out_ref[at, :] = total(i, n, *terms)

    def each(count, body):
        pl.loop(0, count)(body)

    for r in range(4):
        start(load_in(r))
    for i in range(WSLOTS):
        start(load_w(i))
    barrier = pltpu.get_barrier_semaphore()
    pl.semaphore_signal(barrier, inc=1, device_id={"gy": 1 - core}, device_id_type=MESH)
    pl.semaphore_signal(barrier, inc=1, device_id={"gx": ypeer}, device_id_type=MESH)
    pl.semaphore_signal(barrier, inc=1, device_id={"gx": upward}, device_id_type=MESH)

    @pl.when(mid)
    def _():
        pl.semaphore_signal(barrier, inc=1, device_id={"gx": downward}, device_id_type=MESH)

    act(0)
    pl.semaphore_wait(barrier, 3 + mid.astype(jnp.int32))
    exchange(0).start()
    act(1)
    exchange(1).start()

    for r in range(4):
        exchange(r).wait_recv()
        if r == 0:
            wait(load_w(0))
        mm(0, r)
        to_y(0, 2 * r + 1, r).start()

        @pl.when(end)
        def _():
            end_up(0, 2 * r, r).start()

        if r == 0:
            wait(load_w(1))
        mm(1, r)

        @pl.when(end)
        def _():
            end_up(1, 2 * r, 4 + r).start()

        if r < 2:
            act(r + 2)
            exchange(r + 2).start()
    start(load_w(3))
    start(load_w(4))

    def block(i):
        wait(load_w(i))
        each(4, lambda r: mm(i, r))
        if i >= 2 and i + WSLOTS < 8:
            start(load_w(i + WSLOTS))

    block(2)

    @pl.when(end)
    def _():
        each(8, lambda n: to_y(2, n, 4 + n).start())

    @pl.when(mid)
    def _():
        each(4, lambda n: to_y(2, 2 * n + 1, 20 + n).start())

    block(3)

    @pl.when(end)
    def _():
        def o3b(n):
            add(1, 2 * n + 1, got_y(n))
            end_up(1, 2 * n + 1, 8 + n).start()

        each(4, o3b)

    @pl.when(mid)
    def _():
        def x3a(n):
            add(0, 2 * n, got_lo(n))
            mid_up(0, 2 * n, n).start()

        each(4, x3a)

        def x0a(n):
            add(2, 2 * n, got_up(n))
            mid_down(2, 2 * n, n).start()

        each(4, x0a)

    block(4)

    @pl.when(end)
    def _():
        each(8, lambda n: to_y(4, n, 12 + n).start())

    @pl.when(mid)
    def _():
        each(8, lambda n: to_y(4, n, 4 + n).start())

    block(5)

    @pl.when(mid)
    def _():
        def o3a(n):
            add(1, 2 * n, got_lo(4 + n))
            mid_up(1, 2 * n, 4 + n).start()

        each(4, o3a)

        def o0a(n):
            add(3, 2 * n, got_up(4 + n))
            mid_down(3, 2 * n, 4 + n).start()

        each(4, o0a)

    block(6)

    @pl.when(end)
    def _():
        each(4, lambda n: to_y(6, 2 * n + 1, 20 + n).start())

    @pl.when(mid)
    def _():
        each(8, lambda n: to_y(6, n, 12 + n).start())

    block(7)

    @pl.when(end)
    def _():
        def o2(n):
            add(3, n, got_y(4 + n))
            end_up(3, n, 12 + n).start()

        each(8, o2)

        def x0a(n):
            add(6, 2 * n, got_up(n))
            to_y(6, 2 * n, 24 + n).start()

        each(4, x0a)

        def o1(n):
            add(5, n, got_y(12 + n))
            end_up(5, n, 20 + n).start()

        each(8, o1)
        each(4, lambda n: final(7, 2 * n + 1, got_y(20 + n), got_up(8 + n)))
        each(4, lambda n: final(7, 2 * n, got_y(24 + n), got_up(4 + n)))

    @pl.when(mid)
    def _():
        def ends(n):
            add(1, 2 * n + 1, got_y(n), got_lo(8 + n))
            mid_up(1, 2 * n + 1, 8 + n).start()
            add(3, 2 * n + 1, got_y(20 + n), got_up(8 + n))
            mid_down(3, 2 * n + 1, 8 + n).start()

        each(4, ends)

        def o2(n):
            add(5, n, got_y(4 + n), got_lo(12 + n))
            mid_up(5, n, 12 + n).start()

        each(8, o2)
        each(8, lambda n: final(7, n, got_y(12 + n), got_lo(20 + n), got_up(12 + n)))

    for r in range(4):
        exchange(r).wait_send()

    each(24, lambda s: to_y(0, 0, s).wait_send())

    @pl.when(end)
    def _():
        each(4, lambda s: to_y(0, 0, 24 + s).wait_send())
        each(28, lambda s: end_up(0, 0, s).wait_send())

    @pl.when(mid)
    def _():
        each(20, lambda s: mid_up(0, 0, s).wait_send())
        each(12, lambda s: mid_down(0, 0, s).wait_send())


def fused_shards(gate_pre, up_pre, down_weight):
    rows, half = gate_pre.shape
    depth, width = down_weight.shape
    cols = width // 8
    ch = rows // 8
    dma = pltpu.SemaphoreType.DMA
    return pl.pallas_call(
        kernel,
        out_shape=jax.ShapeDtypeStruct((rows, cols), BF16),
        in_specs=[pl.BlockSpec(memory_space=pl.ANY)] * 3,
        out_specs=pl.BlockSpec(memory_space=pltpu.VMEM),
        scratch_shapes=[
            pltpu.VMEM((rows, half), BF16),
            pltpu.VMEM((rows, half), BF16),
            pltpu.VMEM((rows, depth), BF16),
            pltpu.VMEM((WSLOTS, depth, cols), BF16),
            pltpu.VMEM((8, rows, cols), BF16),
            pltpu.VMEM((28, ch, cols), BF16),
            pltpu.VMEM((28, ch, cols), BF16),
            pltpu.VMEM((20, ch, cols), BF16),
            dma((4,)), dma((4,)), dma((WSLOTS, 2)), dma((4,)), dma((4,)),
            dma((28,)), dma((28,)), dma((28,)), dma((12,)), dma((28,)), dma((20,)),
        ],
        compiler_params=pltpu.CompilerParams(
            collective_id=0, has_side_effects=True, vmem_limit_bytes=60 * 1024 * 1024
        ),
        cost_estimate=pl.CostEstimate(
            flops=2 * rows * depth * width,
            bytes_accessed=2 * (depth * width + 2 * rows * half + rows * cols),
            transcendentals=rows * half,
        ),
    )(gate_pre, up_pre, down_weight)


def solution(mesh):
    placed = (P("rep", ("gx", "gy")), P("rep", ("gx", "gy")), P("gx", "gy"))
    fits = mesh.shape["gx"] == 8 and mesh.shape["gy"] == 2
    return jax.shard_map(
        fused_shards if fits else plain_shards,
        mesh=mesh, in_specs=placed, out_specs=P("rep", ("gy", "gx")), check_vma=False,
    )
```

time: 361 us -> 112 us (0.31)
  waiting for transfers between devices: 301 us -> 0 us
  Pallas kernels: 0 us -> 109 us
  matrix products: 35.6 us -> 0 us
  between operations: 13.4 us -> 0.01 us
  other arithmetic: 7.92 us -> 0 us
    reduce_scatter x1 -> x0, waiting for transfers between devices: 282 us -> none  [shards(): lax.psum_scatter(partial_out, 'gx', scatter_dimension=1, tiled=True)]
    pallas_call x0 -> x1, Pallas kernels: none -> 109 us  [fused_shards(): pl.pallas_call(kernel, out_shape=jax.ShapeDtypeStruct((rows, cols), BF16)...]
    dot_general x1 -> x0, matrix products: 35.6 us -> none  [shards(): jnp.dot(hidden, down_weight, preferred_element_type=jnp.float32)]
    all_gather x1 -> x0, waiting for transfers between devices: 18.9 us -> none  [shards(): lax.all_gather(activate(gate_pre, up_pre), 'gy', axis=1, tiled=True)]
    convert_element_type x2 -> x0, other arithmetic: 7.92 us -> none  [the longest x1 5.23 us: activate(): (jax.nn.silu(gate_vals.astype(jnp.float32)) * up_vals.astype(jnp.float32)...]
  transfers between devices with their start and end apart: 2 -> 0, of which waited for: 2 -> 0; matrix products, arithmetic and copies ran while one was open for 0% -> 0% of each run, Pallas kernels for 0% -> 0%
where the time goes in v1:
time: 112 us
  Pallas kernels  109 us (97%)
  local copies, waits for them, and re-layouts  2.26 us (2%)
    pallas_call x1, Pallas kernels, fused_shards(): pl.pallas_call(kernel, out_shape=jax.ShapeDtypeStruct((rows, cols), BF16)...  109 us
    unnamed x1, local copies, waits for them, and re-layouts  2.26 us

profile of v1, /device:TPU:16, one launch (start us, length us, event | category | flops | bytes accessed | tf_op | source)
XLA Modules:
  0.0 111.6 jit_solution(16651153938782741636)
XLA Ops:
  0.0 109.3 %shard_map.37 = bf16[1024,512]{1,0:T(8,128)(2,1)} custom-call(bf16[1024,1664]{1,0:T(8,128)(2,1)} %gate_ref.1, bf16[1024,1664]{1,0:T(8,128)(2,1)} %up_ref.1, bf16[3328,4096]{1,0:T(8,128)(2,1)} %w_ref.1), custom_call_target="tpu_custom_call" | custom-call | flops 27917287424 | bytes 35127296 | tf_op jit(solution)/shard_map/pallas_call | solution.py:341
  109.3 2.3 %copy.5 = bf16[1024,512]{1,0:T(8,128)(2,1)} copy(bf16[1024,512]{1,0:T(8,128)(2,1)} %shard_map.37) | data formatting | bytes 2097152

commit v2 on v1

--- a/solution.py
+++ b/solution.py
@@ -8,7 +8,7 @@
 from jax.sharding import PartitionSpec as P
 
 MESH = pl.DeviceIdType.MESH
-WSLOTS = 3
+WSLOTS = 6
 F32 = jnp.float32
 BF16 = jnp.bfloat16
 
@@ -74,11 +74,11 @@
         for copy in copies:
             copy.wait()
 
-    def exchange(r):
-        at = pl.ds(r * step, step)
+    def exchange(n):
+        at = pl.ds(n * ch, ch)
         return pltpu.make_async_remote_copy(
             src_ref=hid.at[at, pl.ds(0, half)], dst_ref=hid.at[at, pl.ds(half, half)],
-            send_sem=h_send.at[r], recv_sem=h_recv.at[r],
+            send_sem=h_send.at[n], recv_sem=h_recv.at[n],
             device_id={"gy": 1 - core}, device_id_type=MESH,
         )
 
@@ -109,12 +109,13 @@
             device_id={"gx": downward}, device_id_type=MESH,
         )
 
-    def act(r):
-        wait(load_in(r))
-
-        @pl.loop(0, step // 16)
+    def act(n):
+        if n % 2 == 0:
+            wait(load_in(n // 2))
+
+        @pl.loop(0, ch // 16)
         def _(t):
-            at = pl.ds(pl.multiple_of(r * step + t * 16, 16), 16)
+            at = pl.ds(pl.multiple_of(n * ch + t * 16, 16), 16)
             v = gbuf[at, :].astype(F32)
             h = (0.5 * v) * (jnp.tanh(0.5 * v) + 1.0)
             hid[at, pl.ds(0, half)] = (h * ubuf[at, :].astype(F32)).astype(BF16)
@@ -157,8 +158,6 @@
 
     for r in range(4):
         start(load_in(r))
-    for i in range(WSLOTS):
-        start(load_w(i))
     barrier = pltpu.get_barrier_semaphore()
     pl.semaphore_signal(barrier, inc=1, device_id={"gy": 1 - core}, device_id_type=MESH)
     pl.semaphore_signal(barrier, inc=1, device_id={"gx": ypeer}, device_id_type=MESH)
@@ -171,11 +170,35 @@
     act(0)
     pl.semaphore_wait(barrier, 3 + mid.astype(jnp.int32))
     exchange(0).start()
-    act(1)
-    exchange(1).start()
+    start(load_w(0))
+    for n in range(1, 8):
+        act(n)
+        exchange(n).start()
+        if n < WSLOTS:
+            start(load_w(n))
+
+    def end_merge(r):
+        add(1, 2 * r + 1, got_y(r))
+        end_up(1, 2 * r + 1, 8 + r).start()
+        for n in (2 * r, 2 * r + 1):
+            add(3, n, got_y(4 + n))
+            end_up(3, n, 12 + n).start()
+
+    def up_pair(r):
+        add(0, 2 * r, got_lo(r))
+        mid_up(0, 2 * r, r).start()
+        add(1, 2 * r, got_lo(4 + r))
+        mid_up(1, 2 * r, 4 + r).start()
+
+    def down_pair(r):
+        add(2, 2 * r, got_up(r))
+        mid_down(2, 2 * r, r).start()
+        add(3, 2 * r, got_up(4 + r))
+        mid_down(3, 2 * r, 4 + r).start()
 
     for r in range(4):
-        exchange(r).wait_recv()
+        exchange(2 * r).wait_recv()
+        exchange(2 * r + 1).wait_recv()
         if r == 0:
             wait(load_w(0))
         mm(0, r)
@@ -193,51 +216,28 @@
         def _():
             end_up(1, 2 * r, 4 + r).start()
 
-        if r < 2:
-            act(r + 2)
-            exchange(r + 2).start()
-    start(load_w(3))
-    start(load_w(4))
+        if r == 0:
+            wait(load_w(2))
+        mm(2, r)
+
+        @pl.when(end)
+        def _():
+            to_y(2, 2 * r, 4 + 2 * r).start()
+            to_y(2, 2 * r + 1, 5 + 2 * r).start()
+
+        @pl.when(mid)
+        def _():
+            to_y(2, 2 * r + 1, 20 + r).start()
+
+        if r == 0:
+            wait(load_w(3))
+        mm(3, r)
+    start(load_w(6))
+    start(load_w(7))
 
     def block(i):
         wait(load_w(i))
         each(4, lambda r: mm(i, r))
-        if i >= 2 and i + WSLOTS < 8:
-            start(load_w(i + WSLOTS))
-
-    block(2)
-
-    @pl.when(end)
-    def _():
-        each(8, lambda n: to_y(2, n, 4 + n).start())
-
-    @pl.when(mid)
-    def _():
-        each(4, lambda n: to_y(2, 2 * n + 1, 20 + n).start())
-
-    block(3)
-
-    @pl.when(end)
-    def _():
-        def o3b(n):
-            add(1, 2 * n + 1, got_y(n))
-            end_up(1, 2 * n + 1, 8 + n).start()
-
-        each(4, o3b)
-
-    @pl.when(mid)
-    def _():
-        def x3a(n):
-            add(0, 2 * n, got_lo(n))
-            mid_up(0, 2 * n, n).start()
-
-        each(4, x3a)
-
-        def x0a(n):
-            add(2, 2 * n, got_up(n))
-            mid_down(2, 2 * n, n).start()
-
-        each(4, x0a)
 
     block(4)
 
@@ -248,42 +248,37 @@
     @pl.when(mid)
     def _():
         each(8, lambda n: to_y(4, n, 4 + n).start())
+        each(2, up_pair)
 
     block(5)
 
-    @pl.when(mid)
-    def _():
-        def o3a(n):
-            add(1, 2 * n, got_lo(4 + n))
-            mid_up(1, 2 * n, 4 + n).start()
-
-        each(4, o3a)
-
-        def o0a(n):
-            add(3, 2 * n, got_up(4 + n))
-            mid_down(3, 2 * n, 4 + n).start()
-
-        each(4, o0a)
+    @pl.when(end)
+    def _():
+        each(2, end_merge)
+
+    @pl.when(mid)
+    def _():
+        each(2, down_pair)
+        up_pair(2)
 
     block(6)
 
     @pl.when(end)
     def _():
         each(4, lambda n: to_y(6, 2 * n + 1, 20 + n).start())
+        end_merge(2)
 
     @pl.when(mid)
     def _():
         each(8, lambda n: to_y(6, n, 12 + n).start())
+        up_pair(3)
+        down_pair(2)
 
     block(7)
 
     @pl.when(end)
     def _():
-        def o2(n):
-            add(3, n, got_y(4 + n))
-            end_up(3, n, 12 + n).start()
-
-        each(8, o2)
+        end_merge(3)
 
         def x0a(n):
             add(6, 2 * n, got_up(n))
@@ -301,23 +296,22 @@
 
     @pl.when(mid)
     def _():
-        def ends(n):
-            add(1, 2 * n + 1, got_y(n), got_lo(8 + n))
-            mid_up(1, 2 * n + 1, 8 + n).start()
-            add(3, 2 * n + 1, got_y(20 + n), got_up(8 + n))
-            mid_down(3, 2 * n + 1, 8 + n).start()
-
-        each(4, ends)
-
-        def o2(n):
-            add(5, n, got_y(4 + n), got_lo(12 + n))
-            mid_up(5, n, 12 + n).start()
-
-        each(8, o2)
+        down_pair(3)
+
+        def merge(r):
+            add(1, 2 * r + 1, got_y(r), got_lo(8 + r))
+            mid_up(1, 2 * r + 1, 8 + r).start()
+            for n in (2 * r, 2 * r + 1):
+                add(5, n, got_y(4 + n), got_lo(12 + n))
+                mid_up(5, n, 12 + n).start()
+            add(3, 2 * r + 1, got_y(20 + r), got_up(8 + r))
+            mid_down(3, 2 * r + 1, 8 + r).start()
+
+        each(4, merge)
         each(8, lambda n: final(7, n, got_y(12 + n), got_lo(20 + n), got_up(12 + n)))
 
-    for r in range(4):
-        exchange(r).wait_send()
+    for n in range(8):
+        exchange(n).wait_send()
 
     each(24, lambda s: to_y(0, 0, s).wait_send())
 
@@ -352,7 +346,7 @@
             pltpu.VMEM((28, ch, cols), BF16),
             pltpu.VMEM((28, ch, cols), BF16),
             pltpu.VMEM((20, ch, cols), BF16),
-            dma((4,)), dma((4,)), dma((WSLOTS, 2)), dma((4,)), dma((4,)),
+            dma((4,)), dma((4,)), dma((WSLOTS, 2)), dma((8,)), dma((8,)),
             dma((28,)), dma((28,)), dma((28,)), dma((12,)), dma((28,)), dma((20,)),
         ],
         compiler_params=pltpu.CompilerParams(

time: 112 us -> 93.7 us (0.84)
  Pallas kernels: 109 us -> 91 us
    pallas_call x1, Pallas kernels: 109 us -> 91 us  [fused_shards(): pl.pallas_call(kernel, out_shape=jax.ShapeDtypeStruct((rows, cols), BF16)...]
where the time goes in v2:
time: 93.7 us; the launch traced here: 93.2 us
  Pallas kernels  91 us (97%)
  local copies, waits for them, and re-layouts  2.26 us (2%)
    pallas_call x1, Pallas kernels, fused_shards(): pl.pallas_call(kernel, out_shape=jax.ShapeDtypeStruct((rows, cols), BF16)...  91 us
    unnamed x1, local copies, waits for them, and re-layouts  2.26 us

profile of v2, /device:TPU:16, one launch (start us, length us, event | category | flops | bytes accessed | tf_op | source)
XLA Modules:
  0.0 93.2 jit_solution(3664843739016408157)
XLA Ops:
  0.0 91.0 %shard_map.37 = bf16[1024,512]{1,0:T(8,128)(2,1)} custom-call(bf16[1024,1664]{1,0:T(8,128)(2,1)} %gate_ref.1, bf16[1024,1664]{1,0:T(8,128)(2,1)} %up_ref.1, bf16[3328,4096]{1,0:T(8,128)(2,1)} %w_ref.1), custom_call_target="tpu_custom_call" | custom-call | flops 27917287424 | bytes 35127296 | tf_op jit(solution)/shard_map/pallas_call | solution.py:335
  91.0 2.3 %copy.5 = bf16[1024,512]{1,0:T(8,128)(2,1)} copy(bf16[1024,512]{1,0:T(8,128)(2,1)} %shard_map.37) | data formatting | bytes 2097152
